TPU v7x, 512 devices: a whole 4x8x8 slice. The times are simulated.
512 devices in a mesh: cand: 32 (over x_lo, y, core), ref: 16 (over z, x_hi).
Axes of the slice: x: 4 (x_hi: 2, x_lo: 2; x = x_hi * 2 + x_lo), y: 8, z: 8, core: 2. Of those that a mesh axis runs over, the one named last changes fastest.
Arguments:
- cand_factor: float32 [32768, 512], P('cand'), may hold values from -6 to 6
- ref_factor: float32 [8192, 512], P('ref'), may hold values from -6 to 6
- cand_plan: float32 [32768, 128], P('cand'), may hold values from 0.0625 to 16
- ref_plan: float32 [8192, 128], P('ref'), may hold values from 0.0625 to 16
- weights: float32 [128], replicated, may hold values from 0.5 to 2
Outputs:
- new_cand_plan: float32 [32768, 128], P('cand')
- new_ref_plan: float32 [8192, 128], P('ref')
- new_weights: float32 [128], replicated
All inputs are finite; a program needn't handle non-finite values. Where the computation divides by a largest or mean magnitude, that divisor is 1e-20 or more.
Results may differ from a plain program's by a relative error of at most 0.00019.
Values sent between devices are 32-bit elements; how exact they have to be, the bound alone decides.
A program may use at most 64 MiB of HBM per device.

v0:
```python
import jax
import jax.numpy as jnp
from jax import lax
from jax.sharding import PartitionSpec as P

ITERS = 3


step_size = 3.0
tiny_value = 1e-06


def contract_rows(left, right):
    return lax.dot_general(
        left,
        right,
        (((0,), (0,)), ((), ())),
        precision=lax.Precision.HIGHEST,
        preferred_element_type=jnp.float32,
    )


def on_device(cand_factor, ref_factor, cand_plan, ref_plan, weights):
    cand_count = lax.axis_size("cand")
    ref_count = lax.axis_size("ref")
    cand_total = cand_factor.shape[0] * cand_count
    ref_total = ref_factor.shape[0] * ref_count
    rank_width = weights.shape[0]
    cand_block, cand_local = (cand_factor, cand_plan)
    ref_block, ref_local = (ref_factor, ref_plan)
    cand_partial = contract_rows(cand_block, cand_local) / cand_total
    ref_partial = contract_rows(ref_block, ref_local) / ref_total
    cand_moment = lax.psum(cand_partial, "cand")
    ref_moment = lax.psum(ref_partial, "ref")
    grad_cand = jnp.dot(cand_block, ref_moment, precision=lax.Precision.HIGHEST) / weights[None, :]
    grad_ref = jnp.dot(ref_block, cand_moment, precision=lax.Precision.HIGHEST) / weights[None, :]
    grad_weights = -jnp.sum(cand_moment * ref_moment, axis=0) / (weights * weights)
    local_top = jnp.maximum(jnp.max(jnp.abs(grad_cand)), jnp.max(jnp.abs(grad_ref)))
    global_top = lax.pmax(local_top, ("cand", "ref"))
    top = jnp.maximum(global_top, jnp.max(jnp.abs(grad_weights))) + tiny_value
    kernel_cand = cand_local * jnp.exp(-step_size * grad_cand / top)
    kernel_ref = ref_local * jnp.exp(-step_size * grad_ref / top)
    kernel_weights = weights * jnp.exp(-step_size * grad_weights / top)
    scale_cand = jnp.ones((rank_width,), jnp.float32)
    scale_ref = jnp.ones((rank_width,), jnp.float32)
    for repeat_index in range(ITERS):
        row_cand = rank_width / jnp.dot(kernel_cand, scale_cand, precision=lax.Precision.HIGHEST)
        row_ref = rank_width / jnp.dot(kernel_ref, scale_ref, precision=lax.Precision.HIGHEST)
        cand_mass_part = (
            jnp.dot(row_cand, kernel_cand, precision=lax.Precision.HIGHEST) / cand_total
        )
        ref_mass_part = jnp.dot(row_ref, kernel_ref, precision=lax.Precision.HIGHEST) / ref_total
        mass_cand = lax.psum(cand_mass_part, "cand")
        mass_ref = lax.psum(ref_mass_part, "ref")
        new_weights = jnp.cbrt(kernel_weights * scale_cand * mass_cand * scale_ref * mass_ref)
        scale_cand = new_weights / mass_cand
        scale_ref = new_weights / mass_ref
    new_cand_plan = row_cand[:, None] * kernel_cand * scale_cand[None, :]
    new_ref_plan = row_ref[:, None] * kernel_ref * scale_ref[None, :]
    return (new_cand_plan, new_ref_plan, new_weights)


def solution(mesh):
    in_specs = (P("cand", None), P("ref", None), P("cand", None), P("ref", None), P())
    out_specs = (P("cand", None), P("ref", None), P())
    return jax.shard_map(
        on_device, mesh=mesh, in_specs=in_specs, out_specs=out_specs, check_vma=False
    )
```

profile of v0, /device:TPU:1, one launch (start us, length us, event | category | flops | bytes accessed | tf_op | source)
XLA Modules:
  0.0 797.6 jit_solution(4981073290394891448)
XLA Ops:
  7.2 0.0 copy-start
  7.2 0.0 copy-start.2
  7.2 0.0 all-reduce.3.cloned.1.call-start
  7.2 3.9 convolution_multiply_fusion.1
  11.2 0.0 all-reduce.3.cloned.1.call-update
  11.2 0.0 all-reduce.5.cloned.1.call-start
  11.2 0.0 copy-done
  11.3 0.0 copy-done.2
  11.3 4.1 convolution_multiply_fusion
  15.4 0.0 all-reduce.5.cloned.1.call-update
  15.4 0.0 copy-done.3
  15.4 0.8 copy.9
  16.3 154.0 %all-reduce.3.cloned.1.call-done = f32[512,128]{1,0:T(8,128)} async-done(((f32[512,128]{1,0:T(8,128)}), f32[512,128]{1,0:T(8,128)}) %all-reduce.3.cloned.1.call-update) | async-done | bytes 262160 | tf_op jit(solution)/shard_map/psum | solution.py:34
  170.3 0.0 copy-done.5
  170.3 4.3 abs_reduce_fusion
  174.6 231.7 %all-reduce.5.cloned.1.call-done = f32[512,128]{1,0:T(8,128)} async-done(((f32[512,128]{1,0:T(8,128)}), f32[512,128]{1,0:T(8,128)}) %all-reduce.5.cloned.1.call-update) | async-done | bytes 262160 | tf_op jit(solution)/shard_map/psum | solution.py:33
  406.2 0.0 copy-done.1
  406.2 3.3 abs_reduce_fusion.1
  410.9 1.2 copy.8
  412.1 100.0 %pmax.7 = f32[]{:T(128)} all-reduce(f32[]{:T(128)S(6)} %max.8), channel_id=1, replica_groups=mesh['cand'=32,'ref'=16] {'cand','ref'}, use_global_device_ids=true, to_apply=%region_4.0 | all-reduce | flops 1 | bytes 8 | tf_op jit(solution)/shard_map/pmax | solution.py:39
  512.1 0.0 copy-done.4
  512.1 1.0 multiply_reduce_fusion
  513.1 0.7 abs_reduce_fusion.2
  515.1 1.1 bitcast_multiply_fusion.1
  516.2 0.3 fusion.14
  516.4 0.3 fusion
  516.7 31.0 %psum.59 = f32[128]{0:T(128)S(1)} all-reduce(f32[128]{0:T(128)S(1)} %fusion), channel_id=1, replica_groups=mesh['cand'=32,'ref'=16] {'ref'}, use_global_device_ids=true, to_apply=%region_8.0 | all-reduce | flops 128 | bytes 1024 | tf_op jit(solution)/shard_map/psum | solution.py:54
  547.7 1.1 bitcast_multiply_fusion
  548.9 0.4 fusion.16
  549.3 0.5 fusion.5
  549.8 60.2 %psum.58 = f32[128]{0:T(128)S(1)} all-reduce(f32[128]{0:T(128)S(1)} %fusion.5), channel_id=1, replica_groups=mesh['cand'=32,'ref'=16] {'cand'}, use_global_device_ids=true, to_apply=%region_7.0 | all-reduce | flops 128 | bytes 1024 | tf_op jit(solution)/shard_map/psum | solution.py:53
  610.0 0.3 fusion.10
  610.3 0.4 fusion.12
  610.7 0.3 fusion.1
  611.0 31.4 %psum.61 = f32[128]{0:T(128)S(1)} all-reduce(f32[128]{0:T(128)S(1)} %fusion.1), channel_id=1, replica_groups=mesh['cand'=32,'ref'=16] {'ref'}, use_global_device_ids=true, to_apply=%region_10.0 | all-reduce | flops 128 | bytes 1024 | tf_op jit(solution)/shard_map/psum | solution.py:54
  642.3 0.5 fusion.4
  642.9 60.2 %psum.60 = f32[128]{0:T(128)S(1)} all-reduce(f32[128]{0:T(128)S(1)} %fusion.4), channel_id=1, replica_groups=mesh['cand'=32,'ref'=16] {'cand'}, use_global_device_ids=true, to_apply=%region_9.0 | all-reduce | flops 128 | bytes 1024 | tf_op jit(solution)/shard_map/psum | solution.py:53
  703.1 0.4 fusion.8
  703.5 0.5 fusion.3
  704.1 53.0 %psum.62 = f32[128]{0:T(128)S(1)} all-reduce(f32[128]{0:T(128)S(1)} %fusion.3), channel_id=1, replica_groups=mesh['cand'=32,'ref'=16] {'cand'}, use_global_device_ids=true, to_apply=%region_11.0 | all-reduce | flops 128 | bytes 1024 | tf_op jit(solution)/shard_map/psum | solution.py:53
  757.1 0.3 fusion.6
  757.3 0.3 fusion.2
  757.6 31.0 %psum.63 = f32[128]{0:T(128)S(1)} all-reduce(f32[128]{0:T(128)S(1)} %fusion.2), channel_id=1, replica_groups=mesh['cand'=32,'ref'=16] {'ref'}, use_global_device_ids=true, to_apply=%region_12.0 | all-reduce | flops 128 | bytes 1024 | tf_op jit(solution)/shard_map/psum | solution.py:54
  788.7 0.1 multiply_multiply_fusion.1
  788.8 0.8 copy.11
  789.6 0.1 multiply_multiply_fusion
  789.7 1.0 copy.10
  790.7 0.0 copy-done.6
  (16 shorter events, 0.1 us)
Async XLA Ops:
  7.2 4.1 copy-start
  7.2 4.1 copy-start.2
  7.2 163.1 %all-reduce.3.cloned.1.call-start = ((), (), s32[]{:S(2)}) async-start(), calls=%async_computation | async-start | bytes 524288 | tf_op jit(solution)/shard_map/psum | solution.py:34
  11.2 4.3 copy-start.3
  11.2 159.1 %copy-start.5 = (f32[128]{0:T(128)S(1)}, f32[128]{0:T(128)}, u32[]{:S(2)}) copy-start(f32[128]{0:T(128)} %param.9) | copy-start | bytes 1540
  11.2 395.0 %all-reduce.5.cloned.1.call-start = ((), (), s32[]{:S(2)}) async-start(), calls=%async_computation.1 | async-start | bytes 524288 | tf_op jit(solution)/shard_map/psum | solution.py:33
  15.4 390.8 %copy-start.1 = (f32[512,512]{1,0:T(8,128)S(1)}, f32[512,512]{1,0:T(8,128)}, u32[]{:S(2)}) copy-start(f32[512,512]{1,0:T(8,128)} %param.6) | copy-start | bytes 3145732
  170.3 341.8 %copy-start.4 = (f32[512,128]{1,0:T(8,128)S(1)}, f32[512,128]{1,0:T(8,128)}, u32[]{:S(2)}) copy-start(f32[512,128]{1,0:T(8,128)} %all-reduce.3.cloned.1.call-done) | copy-start | bytes 786436
  788.7 2.1 copy-start.6
Sparse Core Ops, SparseCore 0:
  11.5 158.7 all-reduce.2
  173.4 232.7 all-reduce.4
where the time goes:
time: 804 us; the launch traced here: 798 us
  waiting for transfers between devices  386 us (48%)
  blocking collectives  367 us (46%)
  matrix products  20 us (2%)
  between operations  16.7 us (2%)
    psum x1, waiting for transfers between devices, on_device(): cand_moment = lax.psum(cand_partial, 'cand')  232 us
    psum x3, blocking collectives, on_device(): mass_cand = lax.psum(cand_mass_part, 'cand')  173 us
    psum x1, waiting for transfers between devices, on_device(): ref_moment = lax.psum(ref_partial, 'ref')  154 us
    pmax x1, blocking collectives, on_device(): global_top = lax.pmax(local_top, ('cand', 'ref'))  100 us
    psum x3, blocking collectives, on_device(): mass_ref = lax.psum(ref_mass_part, 'ref')  93.4 us
  transfers between devices with their start and end apart: 2, of which 2 were waited for; matrix products, arithmetic and copies ran while one was open for 1% of the time, Pallas kernels for 0%

commit v1 on v0

v1 whole, which is shorter than its diff:
```python
import functools

import jax
import jax.numpy as jnp
from jax import lax
from jax.experimental import pallas as pl
from jax.experimental.pallas import tpu as pltpu
from jax.sharding import PartitionSpec as P

ITERS = 3
STEP_SIZE = 3.0
TINY = 1e-06
LANES = 128
MESH = pl.DeviceIdType.MESH
F32 = jnp.float32
BF16 = jnp.bfloat16


def contract_rows(left, right):
    return lax.dot_general(
        left,
        right,
        (((0,), (0,)), ((), ())),
        precision=lax.Precision.HIGHEST,
        preferred_element_type=F32,
    )


def split(x):
    high = x.astype(BF16)
    return high, (x - high.astype(F32)).astype(BF16)


def cube_root(x):
    y = jnp.exp(jnp.log(x) * (1.0 / 3.0))
    return y - (y * y * y - x) / (3.0 * y * y)


def wait_bytes(ref, sem):
    pltpu.make_async_copy(ref, ref, sem).wait()


def kernel(
    n_cand,
    n_ref,
    cand_factor,
    ref_factor,
    cand_plan,
    ref_plan,
    weights,
    new_cand_plan,
    new_ref_plan,
    new_weights_out,
    cf,
    rf,
    cf_block,
    rf_block,
    cp,
    rp,
    cf_high,
    cf_low,
    rf_high,
    rf_low,
    kc,
    kr,
    moment_c,
    moment_r,
    part_c,
    part_r,
    rs_c,
    rs_r,
    ag_c,
    ag_r,
    cand_moment,
    ref_moment,
    out_row,
    in_c,
    in_r,
    load_sems,
    store_sems,
    send_c,
    send_r,
    recv_c,
    recv_r,
):
    c = lax.axis_index("cand")
    r = lax.axis_index("ref")
    rows_c, depth = cf.shape
    rows_r = rf.shape[0]
    width_c = depth // n_ref
    width_r = depth // n_cand
    own = depth // (n_cand * n_ref)

    barrier = pltpu.get_barrier_semaphore()

    def greet_c(i, _):
        pl.semaphore_signal(
            barrier, inc=1, device_id=(lax.rem(c + i, n_cand), r), device_id_type=MESH
        )
        return 0

    def greet_r(i, _):
        pl.semaphore_signal(
            barrier, inc=1, device_id=(c, lax.rem(r + i, n_ref)), device_id_type=MESH
        )
        return 0

    group_c = (r * width_c) // LANES
    group_r = (c * width_r) // LANES
    loads = [
        pltpu.make_async_copy(
            cand_factor.at[:, pl.ds(pl.multiple_of(group_c * LANES, LANES), LANES)],
            cf_block,
            load_sems.at[0],
        ),
        pltpu.make_async_copy(cand_plan, cp, load_sems.at[1]),
        pltpu.make_async_copy(
            ref_factor.at[:, pl.ds(pl.multiple_of(group_r * LANES, LANES), LANES)],
            rf_block,
            load_sems.at[2],
        ),
        pltpu.make_async_copy(ref_plan, rp, load_sems.at[3]),
        pltpu.make_async_copy(cand_factor, cf, load_sems.at[4]),
        pltpu.make_async_copy(ref_factor, rf, load_sems.at[5]),
    ]
    for load in loads:
        load.start()
    lax.fori_loop(1, n_cand, greet_c, 0)
    lax.fori_loop(1, n_ref, greet_r, 0)

    def send_to_c(phase, source, target):
        def body(i, _):
            peer = lax.rem(c + i, n_cand)
            pltpu.make_async_remote_copy(
                src_ref=source(peer),
                dst_ref=target(c),
                send_sem=send_c.at[phase],
                recv_sem=recv_c.at[phase],
                device_id=(peer, r),
                device_id_type=MESH,
            ).start()
            return 0

        lax.fori_loop(1, n_cand, body, 0)

    def send_to_r(phase, source, target):
        def body(i, _):
            peer = lax.rem(r + i, n_ref)
            pltpu.make_async_remote_copy(
                src_ref=source(peer),
                dst_ref=target(r),
                send_sem=send_r.at[phase],
                recv_sem=recv_r.at[phase],
                device_id=(c, peer),
                device_id_type=MESH,
            ).start()
            return 0

        lax.fori_loop(1, n_ref, body, 0)

    loads[0].wait()
    loads[1].wait()
    moment_c[...] = contract_rows(cf_block[...], cp[...]) * (1.0 / (rows_c * n_cand))
    sub_c = pl.multiple_of(r * width_c - group_c * LANES, width_c)
    part_c[...] = moment_c[pl.ds(sub_c, width_c), :].reshape(part_c.shape)
    loads[2].wait()
    loads[3].wait()
    moment_r[...] = contract_rows(rf_block[...], rp[...]) * (1.0 / (rows_r * n_ref))
    sub_r = pl.multiple_of(c * width_r - group_r * LANES, width_r)
    part_r[...] = moment_r[pl.ds(sub_r, width_r), :].reshape(part_r.shape)

    pl.semaphore_wait(barrier, n_cand + n_ref - 2)

    send_to_c(0, lambda peer: part_c.at[peer], lambda me: rs_c.at[me])
    send_to_r(0, lambda peer: part_r.at[peer], lambda me: rs_r.at[me])
    rs_c[c] = part_c[c]
    rs_r[r] = part_r[r]

    loads[4].wait()
    tile = min(rows_c, 64)

    @pl.loop(0, rows_c, step=tile)
    def _(at):
        at = pl.multiple_of(at, tile)
        high, low = split(cf[pl.ds(at, tile), :])
        cf_high[pl.ds(at, tile), :] = high
        cf_low[pl.ds(at, tile), :] = low

    wait_bytes(rs_c.at[pl.ds(0, n_cand - 1)], recv_c.at[0])
    ag_c[c] = jnp.sum(rs_c[...], axis=0)
    send_to_c(1, lambda peer: ag_c.at[c], lambda me: ag_c.at[me])
    wait_bytes(rs_r.at[pl.ds(0, n_ref - 1)], recv_r.at[0])
    ag_r[r] = jnp.sum(rs_r[...], axis=0)
    send_to_r(1, lambda peer: ag_r.at[r], lambda me: ag_r.at[me])

    loads[5].wait()

    @pl.loop(0, rows_r, step=tile)
    def _(at):
        at = pl.multiple_of(at, tile)
        high, low = split(rf[pl.ds(at, tile), :])
        rf_high[pl.ds(at, tile), :] = high
        rf_low[pl.ds(at, tile), :] = low

    def place_c(who):
        return cand_moment.at[pl.ds(pl.multiple_of(who * width_c, width_c), width_c)]

    def place_r(who):
        return ref_moment.at[pl.ds(pl.multiple_of(who * width_r, width_r), width_r)]

    wait_bytes(ag_c.at[pl.ds(0, n_cand - 1)], recv_c.at[1])
    place_c(r)[...] = ag_c[...].reshape(width_c, LANES)
    send_to_r(2, lambda peer: place_c(r), place_c)
    wait_bytes(ag_r.at[pl.ds(0, n_ref - 1)], recv_r.at[1])
    place_r(c)[...] = ag_r[...].reshape(width_r, LANES)
    send_to_c(2, lambda peer: place_r(c), place_r)

    weights_row = weights[...]
    weights_inverse = 1.0 / weights_row

    def gradient(high, low, moment, out, rows):
        right = jnp.concatenate(split(moment[...]), axis=1)
        step = min(rows, 256)

        def body(i, top):
            at = pl.multiple_of(i * step, step)
            both = jnp.dot(
                high[pl.ds(at, step), :], right, preferred_element_type=F32
            ) + jnp.dot(low[pl.ds(at, step), :], right, preferred_element_type=F32)
            grad = (both[:, :LANES] + both[:, LANES:]) * weights_inverse
            out[pl.ds(at, step), :] = grad
            return jnp.maximum(top, jnp.max(jnp.abs(grad), axis=0, keepdims=True))

        return lax.fori_loop(0, rows // step, body, jnp.zeros((1, LANES), F32))

    wait_bytes(ref_moment.at[pl.ds(0, depth - width_r)], recv_c.at[2])
    top_c = gradient(cf_high, cf_low, ref_moment, kc, rows_c)
    wait_bytes(cand_moment.at[pl.ds(0, depth - width_c)], recv_r.at[2])
    top_r = gradient(rf_high, rf_low, cand_moment, kr, rows_r)

    def exchange(phase, row_c, row_r):
        slot = phase - 3
        out_row[slot, 0] = row_c
        out_row[slot, 1] = row_r
        send_to_c(
            phase, lambda peer: out_row.at[slot, 0], lambda me: in_c.at[slot, me]
        )
        send_to_r(
            phase, lambda peer: out_row.at[slot, 1], lambda me: in_r.at[slot, me]
        )
        in_c[slot, c] = row_c
        in_r[slot, r] = row_r
        wait_bytes(in_c.at[slot, pl.ds(0, n_cand - 1)], recv_c.at[phase])
        wait_bytes(in_r.at[slot, pl.ds(0, n_ref - 1)], recv_r.at[phase])
        return in_c[slot], in_r[slot]

    local = jnp.maximum(top_c, top_r)
    tops_c, tops_r = exchange(3, local, local)
    grad_weights = -jnp.sum(
        cand_moment[...] * ref_moment[...], axis=0, keepdims=True
    ) / (weights_row * weights_row)
    tops = jnp.maximum(jnp.max(tops_c, axis=0), jnp.max(tops_r, axis=0))
    tops = jnp.maximum(tops, jnp.abs(grad_weights))
    top = jnp.max(tops, axis=1, keepdims=True) + TINY
    factor = -STEP_SIZE / top
    kernel_weights = weights_row * jnp.exp(grad_weights * factor)

    scale_c = jnp.ones((1, LANES), F32)
    scale_r = jnp.ones((1, LANES), F32)

    def row_pass(k, plan, scale, rows, first, last):
        step = min(rows, 128)

        def body(i, mass):
            at = pl.multiple_of(i * step, step)
            here = pl.ds(at, step)
            if first:
                block = plan[here, :] * jnp.exp(k[here, :] * factor)
                k[here, :] = block
                total = jnp.sum(block, axis=1, keepdims=True)
            else:
                block = k[here, :]
                total = jnp.sum(block * scale, axis=1, keepdims=True)
            scaled = block * (LANES / total)
            if last:
                k[here, :] = scaled
            return mass + jnp.sum(scaled.reshape(step // 8, 8, LANES), axis=0)

        mass = lax.fori_loop(0, rows // step, body, jnp.zeros((8, LANES), F32))
        return jnp.sum(mass, axis=0, keepdims=True)

    for i in range(ITERS):
        first, last = i == 0, i == ITERS - 1
        part_mass_c = row_pass(kc, cp, scale_c, rows_c, first, last)
        part_mass_r = row_pass(kr, rp, scale_r, rows_r, first, last)
        masses_c, masses_r = exchange(4 + i, part_mass_c, part_mass_r)
        mass_c = jnp.sum(masses_c, axis=0) * (1.0 / (rows_c * n_cand))
        mass_r = jnp.sum(masses_r, axis=0) * (1.0 / (rows_r * n_ref))
        new_weights = cube_root(kernel_weights * scale_c * mass_c * scale_r * mass_r)
        scale_c = new_weights / mass_c
        scale_r = new_weights / mass_r

    kc[...] = kc[...] * scale_c
    store_c = pltpu.make_async_copy(kc, new_cand_plan, store_sems.at[0])
    store_c.start()
    kr[...] = kr[...] * scale_r
    store_r = pltpu.make_async_copy(kr, new_ref_plan, store_sems.at[1])
    store_r.start()
    new_weights_out[...] = new_weights

    wait_bytes(part_c.at[pl.ds(0, n_cand - 1)], send_c.at[0])
    wait_bytes(part_r.at[pl.ds(0, n_ref - 1)], send_r.at[0])
    wait_bytes(ag_c.at[pl.ds(0, n_cand - 1)], send_c.at[1])
    wait_bytes(ag_r.at[pl.ds(0, n_ref - 1)], send_r.at[1])
    wait_bytes(cand_moment.at[pl.ds(0, depth - width_c)], send_r.at[2])
    wait_bytes(ref_moment.at[pl.ds(0, depth - width_r)], send_c.at[2])
    for slot in range(1 + ITERS):
        wait_bytes(in_c.at[slot, pl.ds(0, n_cand - 1)], send_c.at[3 + slot])
        wait_bytes(in_r.at[slot, pl.ds(0, n_ref - 1)], send_r.at[3 + slot])
    store_c.wait()
    store_r.wait()


def on_device(n_cand, n_ref, cand_factor, ref_factor, cand_plan, ref_plan, weights):
    rows_c, depth = cand_factor.shape
    rows_r = ref_factor.shape[0]
    rank = weights.shape[0]
    width_c, width_r = depth // n_ref, depth // n_cand
    own = depth // (n_cand * n_ref)
    phases = 4 + ITERS
    anywhere = pl.BlockSpec(memory_space=pl.ANY)
    vmem = pl.BlockSpec(memory_space=pltpu.VMEM)
    new_cand_plan, new_ref_plan, new_weights = pl.pallas_call(
        functools.partial(kernel, n_cand, n_ref),
        out_shape=(
            jax.ShapeDtypeStruct((rows_c, rank), F32),
            jax.ShapeDtypeStruct((rows_r, rank), F32),
            jax.ShapeDtypeStruct((1, rank), F32),
        ),
        in_specs=[anywhere] * 4 + [vmem],
        out_specs=(anywhere, anywhere, vmem),
        scratch_shapes=[
            pltpu.VMEM((rows_c, depth), F32),
            pltpu.VMEM((rows_r, depth), F32),
            pltpu.VMEM((rows_c, LANES), F32),
            pltpu.VMEM((rows_r, LANES), F32),
            pltpu.VMEM((rows_c, rank), F32),
            pltpu.VMEM((rows_r, rank), F32),
            pltpu.VMEM((rows_c, depth), BF16),
            pltpu.VMEM((rows_c, depth), BF16),
            pltpu.VMEM((rows_r, depth), BF16),
            pltpu.VMEM((rows_r, depth), BF16),
            pltpu.VMEM((rows_c, rank), F32),
            pltpu.VMEM((rows_r, rank), F32),
            pltpu.VMEM((LANES, rank), F32),
            pltpu.VMEM((LANES, rank), F32),
            pltpu.VMEM((n_cand, own, rank), F32),
            pltpu.VMEM((n_ref, own, rank), F32),
            pltpu.VMEM((n_cand, own, rank), F32),
            pltpu.VMEM((n_ref, own, rank), F32),
            pltpu.VMEM((n_cand, own, rank), F32),
            pltpu.VMEM((n_ref, own, rank), F32),
            pltpu.VMEM((depth, rank), F32),
            pltpu.VMEM((depth, rank), F32),
            pltpu.VMEM((1 + ITERS, 2, 1, rank), F32),
            pltpu.VMEM((1 + ITERS, n_cand, 1, rank), F32),
            pltpu.VMEM((1 + ITERS, n_ref, 1, rank), F32),
            pltpu.SemaphoreType.DMA((6,)),
            pltpu.SemaphoreType.DMA((2,)),
            pltpu.SemaphoreType.DMA((phases,)),
            pltpu.SemaphoreType.DMA((phases,)),
            pltpu.SemaphoreType.DMA((phases,)),
            pltpu.SemaphoreType.DMA((phases,)),
        ],
        compiler_params=pltpu.CompilerParams(
            collective_id=0, has_side_effects=True, vmem_limit_bytes=32 * 2**20
        ),
    )(cand_factor, ref_factor, cand_plan, ref_plan, weights.reshape(1, rank))
    return new_cand_plan, new_ref_plan, new_weights.reshape(rank)


def solution(mesh):
    in_specs = (P("cand", None), P("ref", None), P("cand", None), P("ref", None), P())
    out_specs = (P("cand", None), P("ref", None), P())
    return jax.shard_map(
        functools.partial(on_device, mesh.shape["cand"], mesh.shape["ref"]),
        mesh=mesh,
        in_specs=in_specs,
        out_specs=out_specs,
        check_vma=False,
    )
```

time: 804 us -> 75.9 us (0.09)
  waiting for transfers between devices: 386 us -> 0 us
  blocking collectives: 367 us -> 0 us
  Pallas kernels: 0 us -> 67.5 us
  matrix products: 20 us -> 0 us
  between operations: 16.7 us -> 0.65 us
    psum x2 -> x0, waiting for transfers between devices: 386 us -> none  [the longest x1 232 us: on_device(): cand_moment = lax.psum(cand_partial, 'cand')]
    psum x6 -> x0, blocking collectives: 267 us -> none  [the longest x3 173 us: on_device(): mass_cand = lax.psum(cand_mass_part, 'cand')]
    pmax x1 -> x0, blocking collectives: 100 us -> none  [on_device(): global_top = lax.pmax(local_top, ('cand', 'ref'))]
    pallas_call x0 -> x1, Pallas kernels: none -> 67.5 us  [on_device(): pl.pallas_call(functools.partial(kernel, n_cand, n_ref), out_shape=(jax.S...]
    dot_general x16 -> x0, matrix products: 20 us -> none  [the longest x2 8.07 us: contract_rows(): lax.dot_general(left, right, (((0,), (0,)), ((), ())), precision=lax.Prec...]
  transfers between devices with their start and end apart: 2 -> 0, of which waited for: 2 -> 0; matrix products, arithmetic and copies ran while one was open for 1% -> 0% of each run, Pallas kernels for 0% -> 0%
where the time goes in v1:
time: 75.9 us; the launch traced here: 75.7 us
  Pallas kernels  67.5 us (89%)
  local copies, waits for them, and re-layouts  7.46 us (10%)
    pallas_call x1, Pallas kernels, on_device(): pl.pallas_call(functools.partial(kernel, n_cand, n_ref), out_shape=(jax.S...  67.5 us
    unnamed x13, local copies, waits for them, and re-layouts  7.46 us

profile of v1, /device:TPU:1, one launch (start us, length us, event | category | flops | bytes accessed | tf_op | source)
XLA Modules:
  0.0 75.7 jit_solution(15920343288331223493)
XLA Ops:
  0.6 0.0 copy-start
  0.6 1.6 %copy-done = f32[1024,512]{1,0:T(8,128)S(1)} copy-done((f32[1024,512]{1,0:T(8,128)S(1)}, f32[1024,512]{1,0:T(8,128)}, u32[]{:S(2)}) %copy-start) | copy-done | bytes 2097176
  2.2 0.0 copy-start.1
  2.2 1.2 %copy-done.1 = f32[512,512]{1,0:T(8,128)S(1)} copy-done((f32[512,512]{1,0:T(8,128)S(1)}, f32[512,512]{1,0:T(8,128)}, u32[]{:S(2)}) %copy-start.1) | copy-done | bytes 1048600
  3.4 0.0 copy-start.2
  3.5 1.0 %copy-done.2 = f32[1024,128]{1,0:T(8,128)S(1)} copy-done((f32[1024,128]{1,0:T(8,128)S(1)}, f32[1024,128]{1,0:T(8,128)}, u32[]{:S(2)}) %copy-start.2) | copy-done | bytes 524312
  4.5 0.0 copy-start.3
  4.5 0.9 %copy-done.3 = f32[512,128]{1,0:T(8,128)S(1)} copy-done((f32[512,128]{1,0:T(8,128)S(1)}, f32[512,128]{1,0:T(8,128)}, u32[]{:S(2)}) %copy-start.3) | copy-done | bytes 262168
  5.4 0.0 copy-start.4
  5.4 0.7 copy-done.4
  6.1 67.5 %shard_map.76 = (f32[1024,128]{1,0:T(8,128)S(1)}, f32[512,128]{1,0:T(8,128)S(1)}, f32[1,128]{1,0:T(1,128)S(1)}) custom-call(f32[1024,512]{1,0:T(8,128)S(1)} %copy-done, f32[512,512]{1,0:T(8,128)S(1)} %copy-done.1, f32[1024,128]{1,0:T(8,128)S(1)} %copy-done.2, f32[512,128]{1,0:T(8,128)S(1)} %copy-done.3, f32[1,128]{1,0:T(1,128)S(1)} %bitcast.2), custom_call_target="tpu_custom_call" | custom-call | tf_op jit(solution)/shard_map/pallas_call | solution.py:333
  73.6 0.8 %copy.11 = f32[1024,128]{1,0:T(8,128)} copy(f32[1024,128]{1,0:T(8,128)S(1)} %get-tuple-element.12) | data formatting | bytes 1048576
  74.4 0.7 copy.12
  75.1 0.5 copy.13
Async XLA Ops:
  0.6 1.6 %copy-start = (f32[1024,512]{1,0:T(8,128)S(1)}, f32[1024,512]{1,0:T(8,128)}, u32[]{:S(2)}) copy-start(f32[1024,512]{1,0:T(8,128)} %cand_factor.1) | copy-start | bytes 6291460
  2.2 1.2 %copy-start.1 = (f32[512,512]{1,0:T(8,128)S(1)}, f32[512,512]{1,0:T(8,128)}, u32[]{:S(2)}) copy-start(f32[512,512]{1,0:T(8,128)} %ref_factor.1) | copy-start | bytes 3145732
  3.4 1.0 %copy-start.2 = (f32[1024,128]{1,0:T(8,128)S(1)}, f32[1024,128]{1,0:T(8,128)}, u32[]{:S(2)}) copy-start(f32[1024,128]{1,0:T(8,128)} %cand_plan.1) | copy-start | bytes 1572868
  4.5 0.9 %copy-start.3 = (f32[512,128]{1,0:T(8,128)S(1)}, f32[512,128]{1,0:T(8,128)}, u32[]{:S(2)}) copy-start(f32[512,128]{1,0:T(8,128)} %ref_plan.1) | copy-start | bytes 786436
  5.4 0.7 copy-start.4

commit v2 on v1

v2 whole, which is shorter than its diff:
```python
import functools

import jax
import jax.numpy as jnp
from jax import lax
from jax.experimental import pallas as pl
from jax.experimental.pallas import tpu as pltpu
from jax.sharding import PartitionSpec as P

ITERS = 3
STEP_SIZE = 3.0
TINY = 1e-06
LANES = 128
MESH = pl.DeviceIdType.MESH
F32 = jnp.float32
BF16 = jnp.bfloat16


def split(x):
    high = x.astype(BF16)
    return high, (x - high.astype(F32)).astype(BF16)


def contract_rows(left, right):
    both = lax.dot_general(
        jnp.concatenate(split(left), axis=1),
        jnp.concatenate(split(right), axis=1),
        (((0,), (0,)), ((), ())),
        preferred_element_type=F32,
    )
    half = left.shape[1]
    return (both[:half, :LANES] + both[half:, LANES:]) + (
        both[half:, :LANES] + both[:half, LANES:]
    )


def cube_root(x):
    y = jnp.exp(jnp.log(x) * (1.0 / 3.0))
    return y - (y * y * y - x) / (3.0 * y * y)


def wait_bytes(ref, sem):
    pltpu.make_async_copy(ref, ref, sem).wait()


def kernel(
    n_cand,
    n_ref,
    cand_factor,
    ref_factor,
    cand_plan,
    ref_plan,
    weights_in,
    scaled_cand,
    scaled_ref,
    rows_out,
    cf,
    rf,
    cf_block,
    rf_block,
    cp,
    rp,
    weights,
    cf_high,
    cf_low,
    rf_high,
    rf_low,
    kc,
    kr,
    moment_c,
    moment_r,
    part_c,
    pair_c,
    sum_c,
    sum_r,
    cand_moment,
    ref_moment,
    out_row,
    in_c,
    in_r,
    load_sems,
    store_sems,
    pair_send,
    pair_recv,
    send_c,
    send_r,
    recv_c,
    recv_r,
):
    c = lax.axis_index("cand")
    r = lax.axis_index("ref")
    n_y, n_z = n_cand // 4, n_ref // 2
    core = lax.rem(c, 2)
    y = lax.rem(c // 2, n_y)
    x_lo = c // (2 * n_y)
    x_hi = lax.rem(r, 2)
    z = r // 2
    spot = x_lo * n_y + y
    side = lax.rem(x_lo + x_hi, 2)
    rows_c, depth = cf.shape
    rows_r = rf.shape[0]
    width_c = depth // n_ref
    width_r = depth // n_cand
    part = width_c // 2
    sibling = 1 - core

    def away(step, size):
        turn = lax.rem(step, 2) * 2 - 1
        return lax.rem(size // 2 + turn * ((step + 1) // 2) + size, size)

    def to_c(flip, offset_y, flip_core):
        new_x = lax.rem(x_lo + flip, 2)
        new_core = lax.rem(core + flip_core, 2)
        return ((new_x * n_y + lax.rem(y + offset_y, n_y)) * 2 + new_core, r)

    def to_r(flip, offset_z):
        new_c = (lax.rem(x_lo + flip, 2) * n_y + y) * 2 + core
        return (new_c, lax.rem(z + offset_z, n_z) * 2 + lax.rem(x_hi + flip, 2))

    def for_all(visit_c, visit_r, cores):
        def body(step, _):
            offset_y = away(step, n_y)
            for flip in (1, 0):
                for flip_core in cores:
                    visit_c(to_c(flip, offset_y, flip_core))
            if n_z == n_y:
                for flip in (1, 0):
                    visit_r(to_r(flip, offset_y))
            return 0

        lax.fori_loop(0, n_y - 1, body, 0)
        if n_z != n_y:

            def body_r(step, _):
                for flip in (1, 0):
                    visit_r(to_r(flip, away(step, n_z)))
                return 0

            lax.fori_loop(0, n_z - 1, body_r, 0)
        for flip_core in cores:
            visit_c(to_c(1, 0, flip_core))
        visit_r(to_r(1, 0))
        if 1 in cores:
            visit_c(to_c(0, 0, 1))

    barrier = pltpu.get_barrier_semaphore()

    def greet(device):
        pl.semaphore_signal(barrier, inc=1, device_id=device, device_id_type=MESH)

    def remote(source, target, send, recv, device):
        return pltpu.make_async_remote_copy(
            src_ref=source,
            dst_ref=target,
            send_sem=send,
            recv_sem=recv,
            device_id=device,
            device_id_type=MESH,
        )

    first_c = r * width_c
    first_r = core * (depth // 2) + (side * n_y + y) * width_r
    group_c = first_c // LANES
    group_r = first_r // LANES
    loads = [
        pltpu.make_async_copy(
            ref_factor.at[:, pl.ds(pl.multiple_of(group_r * LANES, LANES), LANES)],
            rf_block,
            load_sems.at[0],
        ),
        pltpu.make_async_copy(ref_plan, rp, load_sems.at[1]),
        pltpu.make_async_copy(
            cand_factor.at[:, pl.ds(pl.multiple_of(group_c * LANES, LANES), LANES)],
            cf_block,
            load_sems.at[2],
        ),
        pltpu.make_async_copy(cand_plan, cp, load_sems.at[3]),
        pltpu.make_async_copy(weights_in, weights, load_sems.at[4]),
        pltpu.make_async_copy(cand_factor, cf, load_sems.at[5]),
        pltpu.make_async_copy(ref_factor, rf, load_sems.at[6]),
    ]
    for load in loads:
        load.start()
    for_all(greet, greet, (1, 0))

    loads[0].wait()
    loads[1].wait()
    moment_r[...] = contract_rows(rf_block[...], rp[...]) * (1.0 / (rows_r * n_ref))
    sub_r = pl.multiple_of(first_r - group_r * LANES, width_r)
    sum_r[r] = moment_r[pl.ds(sub_r, width_r), :]
    loads[2].wait()
    loads[3].wait()
    moment_c[...] = contract_rows(cf_block[...], cp[...]) * (1.0 / (rows_c * n_cand))
    sub_c = pl.multiple_of(first_c - group_c * LANES, width_c)
    part_c[...] = moment_c[pl.ds(sub_c, width_c), :].reshape(part_c.shape)

    pl.semaphore_wait(barrier, n_cand + n_ref - 2)

    pair = remote(
        part_c.at[sibling], pair_c, pair_send.at[0], pair_recv.at[0], to_c(0, 0, 1)
    )
    pair.start()
    pair.wait_recv()
    sum_c[spot] = part_c[core] + pair_c[...]

    for_all(
        lambda device: remote(
            sum_c.at[spot], sum_c.at[spot], send_c.at[0], recv_c.at[0], device
        ).start(),
        lambda device: remote(
            sum_r.at[r], sum_r.at[r], send_r.at[0], recv_r.at[0], device
        ).start(),
        (0,),
    )

    tile = min(rows_c, rows_r, 64)

    def split_all(factor, high_ref, low_ref, rows):
        @pl.loop(0, rows, step=tile)
        def _(at):
            at = pl.multiple_of(at, tile)
            high, low = split(factor[pl.ds(at, tile), :])
            high_ref[pl.ds(at, tile), :] = high
            low_ref[pl.ds(at, tile), :] = low

    loads[5].wait()
    split_all(cf, cf_high, cf_low, rows_c)
    loads[6].wait()
    split_all(rf, rf_high, rf_low, rows_r)
    loads[4].wait()

    wait_bytes(sum_c.at[pl.ds(0, n_cand // 2 - 1)], recv_c.at[0])
    cand_moment[r, core] = jnp.sum(sum_c[...], axis=0)
    wait_bytes(sum_r.at[pl.ds(0, n_ref - 1)], recv_r.at[0])
    my_slice = ref_moment.at[pl.ds(pl.multiple_of(first_r, width_r), width_r)]
    my_slice[...] = jnp.sum(sum_r[...], axis=0)

    for_all(
        lambda device: remote(
            my_slice, my_slice, send_c.at[1], recv_c.at[1], device
        ).start(),
        lambda device: remote(
            cand_moment.at[r, core],
            cand_moment.at[r, core],
            send_r.at[1],
            recv_r.at[1],
            device,
        ).start(),
        (0,),
    )
    half = depth // 2
    my_half = ref_moment.at[pl.ds(pl.multiple_of(core * half, half), half)]
    wait_bytes(ref_moment.at[pl.ds(0, half - width_r)], recv_c.at[1])
    hand_r = remote(my_half, my_half, pair_send.at[1], pair_recv.at[1], to_c(0, 0, 1))
    hand_r.start()
    wait_bytes(cand_moment.at[pl.ds(0, n_ref - 1), core], recv_r.at[1])
    mine = cand_moment.at[:, pl.ds(core, 1)]
    hand_c = remote(mine, mine, pair_send.at[2], pair_recv.at[2], to_c(0, 0, 1))
    hand_c.start()

    weights_row = weights[...]
    weights_inverse = 1.0 / weights_row

    def gradient(high, low, moment, out, rows):
        right = jnp.concatenate(split(moment), axis=1)
        step = min(rows, 256)

        def body(i, top):
            at = pl.multiple_of(i * step, step)
            both = jnp.dot(
                high[pl.ds(at, step), :], right, preferred_element_type=F32
            ) + jnp.dot(low[pl.ds(at, step), :], right, preferred_element_type=F32)
            grad = (both[:, :LANES] + both[:, LANES:]) * weights_inverse
            out[pl.ds(at, step), :] = grad
            return jnp.maximum(top, jnp.max(jnp.abs(grad), axis=0, keepdims=True))

        return lax.fori_loop(0, rows // step, body, jnp.zeros((1, LANES), F32))

    hand_r.wait_recv()
    top_c = gradient(cf_high, cf_low, ref_moment[...], kc, rows_c)
    hand_c.wait_recv()
    all_cand_moment = cand_moment[...].reshape(depth, LANES)
    top_r = gradient(rf_high, rf_low, all_cand_moment, kr, rows_r)

    def exchange(slot, row_c, row_r):
        out_row[slot, 0] = row_c
        out_row[slot, 1] = row_r
        for_all(
            lambda device: remote(
                out_row.at[slot, 0],
                in_c.at[slot, c],
                send_c.at[2 + slot],
                recv_c.at[2 + slot],
                device,
            ).start(),
            lambda device: remote(
                out_row.at[slot, 1],
                in_r.at[slot, r],
                send_r.at[2 + slot],
                recv_r.at[2 + slot],
                device,
            ).start(),
            (1, 0),
        )
        in_c[slot, c] = row_c
        in_r[slot, r] = row_r
        wait_bytes(in_c.at[slot, pl.ds(0, n_cand - 1)], recv_c.at[2 + slot])
        wait_bytes(in_r.at[slot, pl.ds(0, n_ref - 1)], recv_r.at[2 + slot])
        return in_c[slot], in_r[slot]

    local = jnp.maximum(top_c, top_r)
    tops_c, tops_r = exchange(0, local, local)
    grad_weights = -jnp.sum(
        all_cand_moment * ref_moment[...], axis=0, keepdims=True
    ) / (weights_row * weights_row)
    tops = jnp.maximum(jnp.max(tops_c, axis=0), jnp.max(tops_r, axis=0))
    tops = jnp.maximum(tops, jnp.abs(grad_weights))
    top = jnp.max(tops, axis=1, keepdims=True) + TINY
    factor = -STEP_SIZE / top
    kernel_weights = weights_row * jnp.exp(grad_weights * factor)

    scale_c = jnp.ones((1, LANES), F32)
    scale_r = jnp.ones((1, LANES), F32)

    def row_pass(k, plan, scale, rows, first, last):
        step = min(rows, 128)

        def body(i, mass):
            at = pl.multiple_of(i * step, step)
            here = pl.ds(at, step)
            if first:
                block = plan[here, :] * jnp.exp(k[here, :] * factor)
                k[here, :] = block
                total = jnp.sum(block, axis=1, keepdims=True)
            else:
                block = k[here, :]
                total = jnp.sum(block * scale, axis=1, keepdims=True)
            scaled = block * (LANES / total)
            if last:
                k[here, :] = scaled
            return mass + jnp.sum(scaled.reshape(step // 8, 8, LANES), axis=0)

        mass = lax.fori_loop(0, rows // step, body, jnp.zeros((8, LANES), F32))
        return jnp.sum(mass, axis=0, keepdims=True)

    store_c = pltpu.make_async_copy(kc, scaled_cand, store_sems.at[0])
    store_r = pltpu.make_async_copy(kr, scaled_ref, store_sems.at[1])
    for i in range(ITERS):
        first, last = i == 0, i == ITERS - 1
        part_mass_c = row_pass(kc, cp, scale_c, rows_c, first, last)
        part_mass_r = row_pass(kr, rp, scale_r, rows_r, first, last)
        if last:
            store_c.start()
            store_r.start()
        masses_c, masses_r = exchange(1 + i, part_mass_c, part_mass_r)
        mass_c = jnp.sum(masses_c, axis=0) * (1.0 / (rows_c * n_cand))
        mass_r = jnp.sum(masses_r, axis=0) * (1.0 / (rows_r * n_ref))
        new_weights = cube_root(kernel_weights * scale_c * mass_c * scale_r * mass_r)
        scale_c = new_weights / mass_c
        scale_r = new_weights / mass_r

    rows_out[0:1] = new_weights
    rows_out[1:2] = scale_c
    rows_out[2:3] = scale_r
    store_c.wait()
    store_r.wait()

    pair.wait_send()
    hand_r.wait_send()
    hand_c.wait_send()
    wait_bytes(sum_c.at[pl.ds(0, n_cand // 2 - 1)], send_c.at[0])
    wait_bytes(sum_r.at[pl.ds(0, n_ref - 1)], send_r.at[0])
    wait_bytes(ref_moment.at[pl.ds(0, half - width_r)], send_c.at[1])
    wait_bytes(cand_moment.at[pl.ds(0, n_ref - 1), core], send_r.at[1])
    for slot in range(1 + ITERS):
        wait_bytes(in_c.at[slot, pl.ds(0, n_cand - 1)], send_c.at[2 + slot])
        wait_bytes(in_r.at[slot, pl.ds(0, n_ref - 1)], send_r.at[2 + slot])


def finish(
    scaled_cand, scaled_ref, rows, new_cand_plan, new_ref_plan, new_weights, c, r, w, sems
):
    loads = [
        pltpu.make_async_copy(rows, w, sems.at[0]),
        pltpu.make_async_copy(scaled_ref, r, sems.at[1]),
        pltpu.make_async_copy(scaled_cand, c, sems.at[2]),
    ]
    stores = [
        pltpu.make_async_copy(w.at[pl.ds(0, 1)], new_weights, sems.at[3]),
        pltpu.make_async_copy(r, new_ref_plan, sems.at[4]),
        pltpu.make_async_copy(c, new_cand_plan, sems.at[5]),
    ]
    for load in loads:
        load.start()
    loads[0].wait()
    stores[0].start()
    loads[1].wait()
    r[...] = r[...] * w[2:3]
    stores[1].start()
    loads[2].wait()
    c[...] = c[...] * w[1:2]
    stores[2].start()
    for store in stores:
        store.wait()


def on_device(n_cand, n_ref, cand_factor, ref_factor, cand_plan, ref_plan, weights):
    rows_c, depth = cand_factor.shape
    rows_r = ref_factor.shape[0]
    rank = weights.shape[0]
    width_c, width_r = depth // n_ref, depth // n_cand
    part = width_c // 2
    phases = 3 + ITERS
    hbm = pl.BlockSpec(memory_space=pltpu.HBM)
    vmem = pl.BlockSpec(memory_space=pltpu.VMEM)
    scaled_cand, scaled_ref, rows_out = pl.pallas_call(
        functools.partial(kernel, n_cand, n_ref),
        out_shape=(
            jax.ShapeDtypeStruct((rows_c, rank), F32),
            jax.ShapeDtypeStruct((rows_r, rank), F32),
            jax.ShapeDtypeStruct((8, rank), F32),
        ),
        in_specs=[hbm] * 5,
        out_specs=(hbm, hbm, vmem),
        scratch_shapes=[
            pltpu.VMEM((rows_c, depth), F32),
            pltpu.VMEM((rows_r, depth), F32),
            pltpu.VMEM((rows_c, LANES), F32),
            pltpu.VMEM((rows_r, LANES), F32),
            pltpu.VMEM((rows_c, rank), F32),
            pltpu.VMEM((rows_r, rank), F32),
            pltpu.VMEM((1, rank), F32),
            pltpu.VMEM((rows_c, depth), BF16),
            pltpu.VMEM((rows_c, depth), BF16),
            pltpu.VMEM((rows_r, depth), BF16),
            pltpu.VMEM((rows_r, depth), BF16),
            pltpu.VMEM((rows_c, rank), F32),
            pltpu.VMEM((rows_r, rank), F32),
            pltpu.VMEM((LANES, rank), F32),
            pltpu.VMEM((LANES, rank), F32),
            pltpu.VMEM((2, part, rank), F32),
            pltpu.VMEM((part, rank), F32),
            pltpu.VMEM((n_cand // 2, part, rank), F32),
            pltpu.VMEM((n_ref, width_r, rank), F32),
            pltpu.VMEM((n_ref, 2, part, rank), F32),
            pltpu.VMEM((depth, rank), F32),
            pltpu.VMEM((1 + ITERS, 2, 1, rank), F32),
            pltpu.VMEM((1 + ITERS, n_cand, 1, rank), F32),
            pltpu.VMEM((1 + ITERS, n_ref, 1, rank), F32),
            pltpu.SemaphoreType.DMA((7,)),
            pltpu.SemaphoreType.DMA((2,)),
            pltpu.SemaphoreType.DMA((3,)),
            pltpu.SemaphoreType.DMA((3,)),
            pltpu.SemaphoreType.DMA((phases,)),
            pltpu.SemaphoreType.DMA((phases,)),
            pltpu.SemaphoreType.DMA((phases,)),
            pltpu.SemaphoreType.DMA((phases,)),
        ],
        compiler_params=pltpu.CompilerParams(
            collective_id=0, has_side_effects=True, vmem_limit_bytes=60 * 2**20
        ),
    )(cand_factor, ref_factor, cand_plan, ref_plan, weights.reshape(1, rank))
    new_cand_plan, new_ref_plan, new_weights = pl.pallas_call(
        finish,
        out_shape=(
            jax.ShapeDtypeStruct((rows_c, rank), F32),
            jax.ShapeDtypeStruct((rows_r, rank), F32),
            jax.ShapeDtypeStruct((1, rank), F32),
        ),
        in_specs=[hbm] * 3,
        out_specs=(hbm, hbm, hbm),
        scratch_shapes=[
            pltpu.VMEM((rows_c, rank), F32),
            pltpu.VMEM((rows_r, rank), F32),
            pltpu.VMEM((8, rank), F32),
            pltpu.SemaphoreType.DMA((6,)),
        ],
        compiler_params=pltpu.CompilerParams(vmem_limit_bytes=60 * 2**20),
    )(scaled_cand, scaled_ref, rows_out)
    return new_cand_plan, new_ref_plan, new_weights.reshape(rank)


def solution(mesh):
    in_specs = (P("cand", None), P("ref", None), P("cand", None), P("ref", None), P())
    out_specs = (P("cand", None), P("ref", None), P())
    return jax.shard_map(
        functools.partial(on_device, mesh.shape["cand"], mesh.shape["ref"]),
        mesh=mesh,
        in_specs=in_specs,
        out_specs=out_specs,
        check_vma=False,
    )
```

time: 75.9 us -> 60.4 us (0.80)
  Pallas kernels: 67.5 us -> 59.6 us
  local copies, waits for them, and re-layouts: 7.46 us -> 0 us
    pallas_call x1, Pallas kernels: 67.5 us -> 57.6 us  [on_device(): pl.pallas_call(functools.partial(kernel, n_cand, n_ref), out_shape=(jax.S...]
    unnamed x13 -> x0, local copies, waits for them, and re-layouts: 7.46 us -> none
    pallas_call x0 -> x1, Pallas kernels: none -> 2.01 us  [on_device(): pl.pallas_call(finish, out_shape=(jax.ShapeDtypeStruct((rows_c, rank), F3...]
where the time goes in v2:
time: 60.4 us; the launch traced here: 60.2 us
  Pallas kernels  59.6 us (99%)
  between operations  0.64 us (1%)
    pallas_call x1, Pallas kernels, on_device(): pl.pallas_call(functools.partial(kernel, n_cand, n_ref), out_shape=(jax.S...  57.6 us
    pallas_call x1, Pallas kernels, on_device(): pl.pallas_call(finish, out_shape=(jax.ShapeDtypeStruct((rows_c, rank), F3...  2.01 us

profile of v2, /device:TPU:1, one launch (start us, length us, event | category | flops | bytes accessed | tf_op | source)
XLA Modules:
  0.0 60.2 jit_solution(5526978597812250908)
XLA Ops:
  0.6 57.6 %shard_map.76 = (f32[1024,128]{1,0:T(8,128)}, f32[512,128]{1,0:T(8,128)}, f32[8,128]{1,0:T(8,128)}) custom-call(f32[1024,512]{1,0:T(8,128)} %cand_factor.1, f32[512,512]{1,0:T(8,128)} %ref_factor.1, f32[1024,128]{1,0:T(8,128)} %cand_plan.1, f32[512,128]{1,0:T(8,128)} %ref_plan.1, f32[1,128]{1,0:T(1,128)} %bitcast.2), custom_call_target="tpu_custom_call" | custom-call | tf_op jit(solution)/shard_map/pallas_call | solution.py:416
  58.2 2.0 %shard_map.77 = (f32[1024,128]{1,0:T(8,128)}, f32[512,128]{1,0:T(8,128)}, f32[1,128]{1,0:T(1,128)}) custom-call(f32[1024,128]{1,0:T(8,128)} %get-tuple-element.9.scaled_cand, f32[512,128]{1,0:T(8,128)} %get-tuple-element.10.scaled_ref, f32[8,128]{1,0:T(8,128)} %get-tuple-element.11.rows), custom_call_target="tpu_custom_call" | custom-call | tf_op jit(solution)/shard_map/pallas_call | solution.py:463

commit v3 on v2

--- a/solution.py
+++ b/solution.py
@@ -56,8 +56,6 @@
     rows_out,
     cf,
     rf,
-    cf_block,
-    rf_block,
     cp,
     rp,
     weights,
@@ -79,7 +77,7 @@
     in_c,
     in_r,
     load_sems,
-    store_sems,
+    rest_sems,
     pair_send,
     pair_recv,
     send_c,
@@ -97,8 +95,10 @@
     z = r // 2
     spot = x_lo * n_y + y
     side = lax.rem(x_lo + x_hi, 2)
-    rows_c, depth = cf.shape
-    rows_r = rf.shape[0]
+    groups, rows_c, _ = cf.shape
+    rows_r = rf.shape[1]
+    depth = groups * LANES
+    half = depth // 2
     width_c = depth // n_ref
     width_r = depth // n_cand
     part = width_c // 2
@@ -162,35 +162,39 @@
     first_r = core * (depth // 2) + (side * n_y + y) * width_r
     group_c = first_c // LANES
     group_r = first_r // LANES
+    for_all(greet, greet, (1, 0))
+
+    def columns(factor, group, target, sem):
+        at = pl.ds(pl.multiple_of(group * LANES, LANES), LANES)
+        return pltpu.make_async_copy(factor.at[:, at], target.at[group], sem)
+
     loads = [
-        pltpu.make_async_copy(
-            ref_factor.at[:, pl.ds(pl.multiple_of(group_r * LANES, LANES), LANES)],
-            rf_block,
-            load_sems.at[0],
-        ),
+        columns(ref_factor, group_r, rf, load_sems.at[0]),
         pltpu.make_async_copy(ref_plan, rp, load_sems.at[1]),
-        pltpu.make_async_copy(
-            cand_factor.at[:, pl.ds(pl.multiple_of(group_c * LANES, LANES), LANES)],
-            cf_block,
-            load_sems.at[2],
-        ),
+        columns(cand_factor, group_c, cf, load_sems.at[2]),
         pltpu.make_async_copy(cand_plan, cp, load_sems.at[3]),
         pltpu.make_async_copy(weights_in, weights, load_sems.at[4]),
-        pltpu.make_async_copy(cand_factor, cf, load_sems.at[5]),
-        pltpu.make_async_copy(ref_factor, rf, load_sems.at[6]),
     ]
     for load in loads:
         load.start()
-    for_all(greet, greet, (1, 0))
+    rest = [
+        columns(cand_factor, lax.rem(group_c + i, groups), cf, rest_sems.at[0, i])
+        for i in range(1, groups)
+    ] + [
+        columns(ref_factor, lax.rem(group_r + i, groups), rf, rest_sems.at[1, i])
+        for i in range(1, groups)
+    ]
 
     loads[0].wait()
     loads[1].wait()
-    moment_r[...] = contract_rows(rf_block[...], rp[...]) * (1.0 / (rows_r * n_ref))
+    moment_r[...] = contract_rows(rf[group_r], rp[...]) * (1.0 / (rows_r * n_ref))
     sub_r = pl.multiple_of(first_r - group_r * LANES, width_r)
     sum_r[r] = moment_r[pl.ds(sub_r, width_r), :]
     loads[2].wait()
     loads[3].wait()
-    moment_c[...] = contract_rows(cf_block[...], cp[...]) * (1.0 / (rows_c * n_cand))
+    for load in rest:
+        load.start()
+    moment_c[...] = contract_rows(cf[group_c], cp[...]) * (1.0 / (rows_c * n_cand))
     sub_c = pl.multiple_of(first_c - group_c * LANES, width_c)
     part_c[...] = moment_c[pl.ds(sub_c, width_c), :].reshape(part_c.shape)
 
@@ -213,19 +217,21 @@
         (0,),
     )
 
-    tile = min(rows_c, rows_r, 64)
-
     def split_all(factor, high_ref, low_ref, rows):
-        @pl.loop(0, rows, step=tile)
-        def _(at):
-            at = pl.multiple_of(at, tile)
-            high, low = split(factor[pl.ds(at, tile), :])
-            high_ref[pl.ds(at, tile), :] = high
-            low_ref[pl.ds(at, tile), :] = low
-
-    loads[5].wait()
+        tile = min(rows, 128)
+        for group in range(groups):
+            side_of, at = divmod(group * LANES, half)
+
+            @pl.loop(0, rows // tile)
+            def _(i):
+                here = pl.ds(pl.multiple_of(i * tile, tile), tile)
+                high, low = split(factor[group, here, :])
+                high_ref[side_of, here, at : at + LANES] = high
+                low_ref[side_of, here, at : at + LANES] = low
+
+    for load in rest:
+        load.wait()
     split_all(cf, cf_high, cf_low, rows_c)
-    loads[6].wait()
     split_all(rf, rf_high, rf_low, rows_r)
     loads[4].wait()
 
@@ -248,7 +254,6 @@
         ).start(),
         (0,),
     )
-    half = depth // 2
     my_half = ref_moment.at[pl.ds(pl.multiple_of(core * half, half), half)]
     wait_bytes(ref_moment.at[pl.ds(0, half - width_r)], recv_c.at[1])
     hand_r = remote(my_half, my_half, pair_send.at[1], pair_recv.at[1], to_c(0, 0, 1))
@@ -261,26 +266,47 @@
     weights_row = weights[...]
     weights_inverse = 1.0 / weights_row
 
-    def gradient(high, low, moment, out, rows):
-        right = jnp.concatenate(split(moment), axis=1)
-        step = min(rows, 256)
-
-        def body(i, top):
-            at = pl.multiple_of(i * step, step)
-            both = jnp.dot(
-                high[pl.ds(at, step), :], right, preferred_element_type=F32
-            ) + jnp.dot(low[pl.ds(at, step), :], right, preferred_element_type=F32)
-            grad = (both[:, :LANES] + both[:, LANES:]) * weights_inverse
-            out[pl.ds(at, step), :] = grad
-            return jnp.maximum(top, jnp.max(jnp.abs(grad), axis=0, keepdims=True))
-
-        return lax.fori_loop(0, rows // step, body, jnp.zeros((1, LANES), F32))
-
+    def right_side(moment):
+        return jnp.concatenate(split(moment), axis=1)
+
+    def product(high, low, which, here, right):
+        both = jnp.dot(
+            high[which, here, :], right, preferred_element_type=F32
+        ) + jnp.dot(low[which, here, :], right, preferred_element_type=F32)
+        return both[:, :LANES] + both[:, LANES:]
+
+    def tiles(rows, step):
+        return [pl.ds(at, step) for at in range(0, rows, step)]
+
+    def peak(top, grad):
+        return jnp.maximum(
+            top, jnp.max(jnp.abs(grad).reshape(-1, 8, LANES), axis=0)
+        )
+
+    step_c, step_r = min(rows_c, 256), min(rows_r, 256)
+    right = right_side(my_half[...])
+    for here in tiles(rows_c, step_c):
+        kc[here, :] = product(cf_high, cf_low, core, here, right)
+    tops = jnp.zeros((8, LANES), F32)
     hand_r.wait_recv()
-    top_c = gradient(cf_high, cf_low, ref_moment[...], kc, rows_c)
+    other = ref_moment[pl.ds(pl.multiple_of(sibling * half, half), half), :]
+    right = right_side(other)
+    for here in tiles(rows_c, step_c):
+        grad = kc[here, :] + product(cf_high, cf_low, sibling, here, right)
+        grad = grad * weights_inverse
+        kc[here, :] = grad
+        tops = peak(tops, grad)
     hand_c.wait_recv()
     all_cand_moment = cand_moment[...].reshape(depth, LANES)
-    top_r = gradient(rf_high, rf_low, all_cand_moment, kr, rows_r)
+    rights = [right_side(all_cand_moment[:half]), right_side(all_cand_moment[half:])]
+    for here in tiles(rows_r, step_r):
+        grad = product(rf_high, rf_low, 0, here, rights[0]) + product(
+            rf_high, rf_low, 1, here, rights[1]
+        )
+        grad = grad * weights_inverse
+        kr[here, :] = grad
+        tops = peak(tops, grad)
+    local = jnp.max(tops, axis=0, keepdims=True)
 
     def exchange(slot, row_c, row_r):
         out_row[slot, 0] = row_c
@@ -308,7 +334,6 @@
         wait_bytes(in_r.at[slot, pl.ds(0, n_ref - 1)], recv_r.at[2 + slot])
         return in_c[slot], in_r[slot]
 
-    local = jnp.maximum(top_c, top_r)
     tops_c, tops_r = exchange(0, local, local)
     grad_weights = -jnp.sum(
         all_cand_moment * ref_moment[...], axis=0, keepdims=True
@@ -322,12 +347,10 @@
     scale_c = jnp.ones((1, LANES), F32)
     scale_r = jnp.ones((1, LANES), F32)
 
-    def row_pass(k, plan, scale, rows, first, last):
-        step = min(rows, 128)
-
-        def body(i, mass):
-            at = pl.multiple_of(i * step, step)
-            here = pl.ds(at, step)
+    def row_pass(k, plan, scale, first, to):
+        rows = k.shape[0]
+        mass = jnp.zeros((8, LANES), F32)
+        for here in tiles(rows, min(rows, 128)):
             if first:
                 block = plan[here, :] * jnp.exp(k[here, :] * factor)
                 k[here, :] = block
@@ -336,22 +359,15 @@
                 block = k[here, :]
                 total = jnp.sum(block * scale, axis=1, keepdims=True)
             scaled = block * (LANES / total)
-            if last:
-                k[here, :] = scaled
-            return mass + jnp.sum(scaled.reshape(step // 8, 8, LANES), axis=0)
-
-        mass = lax.fori_loop(0, rows // step, body, jnp.zeros((8, LANES), F32))
+            if to is not None:
+                to[here, :] = scaled
+            mass = mass + jnp.sum(scaled.reshape(-1, 8, LANES), axis=0)
         return jnp.sum(mass, axis=0, keepdims=True)
 
-    store_c = pltpu.make_async_copy(kc, scaled_cand, store_sems.at[0])
-    store_r = pltpu.make_async_copy(kr, scaled_ref, store_sems.at[1])
     for i in range(ITERS):
         first, last = i == 0, i == ITERS - 1
-        part_mass_c = row_pass(kc, cp, scale_c, rows_c, first, last)
-        part_mass_r = row_pass(kr, rp, scale_r, rows_r, first, last)
-        if last:
-            store_c.start()
-            store_r.start()
+        part_mass_c = row_pass(kc, cp, scale_c, first, scaled_cand if last else None)
+        part_mass_r = row_pass(kr, rp, scale_r, first, scaled_ref if last else None)
         masses_c, masses_r = exchange(1 + i, part_mass_c, part_mass_r)
         mass_c = jnp.sum(masses_c, axis=0) * (1.0 / (rows_c * n_cand))
         mass_r = jnp.sum(masses_r, axis=0) * (1.0 / (rows_r * n_ref))
@@ -362,8 +378,6 @@
     rows_out[0:1] = new_weights
     rows_out[1:2] = scale_c
     rows_out[2:3] = scale_r
-    store_c.wait()
-    store_r.wait()
 
     pair.wait_send()
     hand_r.wait_send()
@@ -378,28 +392,22 @@
 
 
 def finish(
-    scaled_cand, scaled_ref, rows, new_cand_plan, new_ref_plan, new_weights, c, r, w, sems
+    scaled_cand, scaled_ref, rows, new_cand_plan, new_ref_plan, new_weights, c, r, sems
 ):
-    loads = [
-        pltpu.make_async_copy(rows, w, sems.at[0]),
-        pltpu.make_async_copy(scaled_ref, r, sems.at[1]),
-        pltpu.make_async_copy(scaled_cand, c, sems.at[2]),
+    rows_c, rows_r = c.shape[0], r.shape[0]
+    pieces = [
+        (scaled_cand, c, new_cand_plan, 1, pl.ds(i * rows_c // 2, rows_c // 2))
+        for i in range(2)
+    ] + [(scaled_ref, r, new_ref_plan, 2, pl.ds(0, rows_r))]
+    stores = [
+        pltpu.make_async_copy(rows.at[pl.ds(0, 1)], new_weights, sems.at[len(pieces)])
     ]
-    stores = [
-        pltpu.make_async_copy(w.at[pl.ds(0, 1)], new_weights, sems.at[3]),
-        pltpu.make_async_copy(r, new_ref_plan, sems.at[4]),
-        pltpu.make_async_copy(c, new_cand_plan, sems.at[5]),
-    ]
-    for load in loads:
-        load.start()
-    loads[0].wait()
     stores[0].start()
-    loads[1].wait()
-    r[...] = r[...] * w[2:3]
-    stores[1].start()
-    loads[2].wait()
-    c[...] = c[...] * w[1:2]
-    stores[2].start()
+    for i, (source, scratch, target, row, here) in enumerate(pieces):
+        scratch[here, :] = source[here, :] * rows[row : row + 1]
+        store = pltpu.make_async_copy(scratch.at[here], target.at[here], sems.at[i])
+        store.start()
+        stores.append(store)
     for store in stores:
         store.wait()
 
@@ -412,28 +420,30 @@
     part = width_c // 2
     phases = 3 + ITERS
     hbm = pl.BlockSpec(memory_space=pltpu.HBM)
+    held = [
+        pltpu.with_memory_space_constraint(x, pltpu.HBM)
+        for x in (cand_factor, ref_factor, cand_plan, ref_plan, weights.reshape(1, rank))
+    ]
     vmem = pl.BlockSpec(memory_space=pltpu.VMEM)
     scaled_cand, scaled_ref, rows_out = pl.pallas_call(
         functools.partial(kernel, n_cand, n_ref),
         out_shape=(
-            jax.ShapeDtypeStruct((rows_c, rank), F32),
-            jax.ShapeDtypeStruct((rows_r, rank), F32),
-            jax.ShapeDtypeStruct((8, rank), F32),
+            pltpu.VMEM((rows_c, rank), F32),
+            pltpu.VMEM((rows_r, rank), F32),
+            pltpu.VMEM((8, rank), F32),
         ),
         in_specs=[hbm] * 5,
-        out_specs=(hbm, hbm, vmem),
+        out_specs=(vmem, vmem, vmem),
         scratch_shapes=[
-            pltpu.VMEM((rows_c, depth), F32),
-            pltpu.VMEM((rows_r, depth), F32),
-            pltpu.VMEM((rows_c, LANES), F32),
-            pltpu.VMEM((rows_r, LANES), F32),
+            pltpu.VMEM((depth // LANES, rows_c, LANES), F32),
+            pltpu.VMEM((depth // LANES, rows_r, LANES), F32),
             pltpu.VMEM((rows_c, rank), F32),
             pltpu.VMEM((rows_r, rank), F32),
             pltpu.VMEM((1, rank), F32),
-            pltpu.VMEM((rows_c, depth), BF16),
-            pltpu.VMEM((rows_c, depth), BF16),
-            pltpu.VMEM((rows_r, depth), BF16),
-            pltpu.VMEM((rows_r, depth), BF16),
+            pltpu.VMEM((2, rows_c, depth // 2), BF16),
+            pltpu.VMEM((2, rows_c, depth // 2), BF16),
+            pltpu.VMEM((2, rows_r, depth // 2), BF16),
+            pltpu.VMEM((2, rows_r, depth // 2), BF16),
             pltpu.VMEM((rows_c, rank), F32),
             pltpu.VMEM((rows_r, rank), F32),
             pltpu.VMEM((LANES, rank), F32),
@@ -447,8 +457,8 @@
             pltpu.VMEM((1 + ITERS, 2, 1, rank), F32),
             pltpu.VMEM((1 + ITERS, n_cand, 1, rank), F32),
             pltpu.VMEM((1 + ITERS, n_ref, 1, rank), F32),
-            pltpu.SemaphoreType.DMA((7,)),
-            pltpu.SemaphoreType.DMA((2,)),
+            pltpu.SemaphoreType.DMA((5,)),
+            pltpu.SemaphoreType.DMA((2, depth // LANES)),
             pltpu.SemaphoreType.DMA((3,)),
             pltpu.SemaphoreType.DMA((3,)),
             pltpu.SemaphoreType.DMA((phases,)),
@@ -457,9 +467,9 @@
             pltpu.SemaphoreType.DMA((phases,)),
         ],
         compiler_params=pltpu.CompilerParams(
-            collective_id=0, has_side_effects=True, vmem_limit_bytes=60 * 2**20
+            collective_id=0, has_side_effects=True, vmem_limit_bytes=32 * 2**20
         ),
-    )(cand_factor, ref_factor, cand_plan, ref_plan, weights.reshape(1, rank))
+    )(*held)
     new_cand_plan, new_ref_plan, new_weights = pl.pallas_call(
         finish,
         out_shape=(
@@ -467,16 +477,20 @@
             jax.ShapeDtypeStruct((rows_r, rank), F32),
             jax.ShapeDtypeStruct((1, rank), F32),
         ),
-        in_specs=[hbm] * 3,
+        in_specs=[vmem] * 3,
         out_specs=(hbm, hbm, hbm),
         scratch_shapes=[
             pltpu.VMEM((rows_c, rank), F32),
             pltpu.VMEM((rows_r, rank), F32),
-            pltpu.VMEM((8, rank), F32),
-            pltpu.SemaphoreType.DMA((6,)),
+            pltpu.SemaphoreType.DMA((4,)),
         ],
-        compiler_params=pltpu.CompilerParams(vmem_limit_bytes=60 * 2**20),
-    )(scaled_cand, scaled_ref, rows_out)
+        compiler_params=pltpu.CompilerParams(vmem_limit_bytes=16 * 2**20),
+    )(
+        *(
+            pltpu.with_memory_space_constraint(x, pltpu.VMEM)
+            for x in (scaled_cand, scaled_ref, rows_out)
+        )
+    )
     return new_cand_plan, new_ref_plan, new_weights.reshape(rank)
 
 

time: 60.4 us -> 55.1 us (0.912)
  Pallas kernels: 59.6 us -> 54.3 us
    pallas_call x1, Pallas kernels: 57.6 us -> 53.4 us  [on_device(): pl.pallas_call(functools.partial(kernel, n_cand, n_ref), out_shape=(pltpu...]
    pallas_call x1, Pallas kernels: 2.01 us -> 0.93 us  [on_device(): pl.pallas_call(finish, out_shape=(jax.ShapeDtypeStruct((rows_c, rank), F3...]
where the time goes in v3:
time: 55.1 us; the launch traced here: 54.9 us
  Pallas kernels  54.3 us (99%)
  between operations  0.64 us (1%)
    pallas_call x1, Pallas kernels, on_device(): pl.pallas_call(functools.partial(kernel, n_cand, n_ref), out_shape=(pltpu...  53.4 us

profile of v3, /device:TPU:1, one launch (start us, length us, event | category | flops | bytes accessed | tf_op | source)
XLA Modules:
  0.0 54.9 jit_solution(17461190873250462854)
XLA Ops:
  0.6 53.4 %shard_map.76 = (f32[1024,128]{1,0:T(8,128)S(1)}, f32[512,128]{1,0:T(8,128)S(1)}, f32[8,128]{1,0:T(8,128)S(1)}) custom-call(f32[1024,512]{1,0:T(8,128)} %cand_factor.1, f32[512,512]{1,0:T(8,128)} %ref_factor.1, f32[1024,128]{1,0:T(8,128)} %cand_plan.1, f32[512,128]{1,0:T(8,128)} %ref_plan.1, f32[1,128]{1,0:T(1,128)} %bitcast.2), custom_call_target="tpu_custom_call" | custom-call | tf_op jit(solution)/shard_map/pallas_call | solution.py:428
  54.0 0.9 %shard_map.77 = (f32[1024,128]{1,0:T(8,128)}, f32[512,128]{1,0:T(8,128)}, f32[1,128]{1,0:T(1,128)}) custom-call(f32[1024,128]{1,0:T(8,128)S(1)} %get-tuple-element.9.scaled_cand, f32[512,128]{1,0:T(8,128)S(1)} %get-tuple-element.10.scaled_ref, f32[8,128]{1,0:T(8,128)S(1)} %get-tuple-element.11.rows), custom_call_target="tpu_custom_call" | custom-call | tf_op jit(solution)/shard_map/pallas_call | solution.py:473

commit v4 on v3

--- a/solution.py
+++ b/solution.py
@@ -35,8 +35,17 @@
 
 
 def cube_root(x):
+    slope = 1.0 / (3.0 * x)
     y = jnp.exp(jnp.log(x) * (1.0 / 3.0))
-    return y - (y * y * y - x) / (3.0 * y * y)
+    return y - y * ((y * y * y - x) * slope)
+
+
+def add_up(rows):
+    terms = [rows[i] for i in range(rows.shape[0])]
+    while len(terms) > 1:
+        pairs = [a + b for a, b in zip(terms[::2], terms[1::2])]
+        terms = pairs + terms[len(pairs) * 2 :]
+    return terms[0]
 
 
 def wait_bytes(ref, sem):
@@ -121,15 +130,15 @@
         def body(step, _):
             offset_y = away(step, n_y)
             for flip in (1, 0):
-                for flip_core in cores:
-                    visit_c(to_c(flip, offset_y, flip_core))
-            if n_z == n_y:
-                for flip in (1, 0):
+                if visit_c:
+                    for flip_core in cores:
+                        visit_c(to_c(flip, offset_y, flip_core))
+                if visit_r and n_z == n_y:
                     visit_r(to_r(flip, offset_y))
             return 0
 
         lax.fori_loop(0, n_y - 1, body, 0)
-        if n_z != n_y:
+        if visit_r and n_z != n_y:
 
             def body_r(step, _):
                 for flip in (1, 0):
@@ -137,10 +146,12 @@
                 return 0
 
             lax.fori_loop(0, n_z - 1, body_r, 0)
-        for flip_core in cores:
-            visit_c(to_c(1, 0, flip_core))
-        visit_r(to_r(1, 0))
-        if 1 in cores:
+        if visit_c:
+            for flip_core in cores:
+                visit_c(to_c(1, 0, flip_core))
+        if visit_r:
+            visit_r(to_r(1, 0))
+        if visit_c and 1 in cores:
             visit_c(to_c(0, 0, 1))
 
     barrier = pltpu.get_barrier_semaphore()
@@ -162,8 +173,6 @@
     first_r = core * (depth // 2) + (side * n_y + y) * width_r
     group_c = first_c // LANES
     group_r = first_r // LANES
-    for_all(greet, greet, (1, 0))
-
     def columns(factor, group, target, sem):
         at = pl.ds(pl.multiple_of(group * LANES, LANES), LANES)
         return pltpu.make_async_copy(factor.at[:, at], target.at[group], sem)
@@ -177,6 +186,7 @@
     ]
     for load in loads:
         load.start()
+    for_all(greet, greet, (1, 0))
     rest = [
         columns(cand_factor, lax.rem(group_c + i, groups), cf, rest_sems.at[0, i])
         for i in range(1, groups)
@@ -204,16 +214,21 @@
         part_c.at[sibling], pair_c, pair_send.at[0], pair_recv.at[0], to_c(0, 0, 1)
     )
     pair.start()
+
+    for_all(
+        None,
+        lambda device: remote(
+            sum_r.at[r], sum_r.at[r], send_r.at[0], recv_r.at[0], device
+        ).start(),
+        (0,),
+    )
     pair.wait_recv()
     sum_c[spot] = part_c[core] + pair_c[...]
-
     for_all(
         lambda device: remote(
             sum_c.at[spot], sum_c.at[spot], send_c.at[0], recv_c.at[0], device
         ).start(),
-        lambda device: remote(
-            sum_r.at[r], sum_r.at[r], send_r.at[0], recv_r.at[0], device
-        ).start(),
+        None,
         (0,),
     )
 
@@ -235,16 +250,20 @@
     split_all(rf, rf_high, rf_low, rows_r)
     loads[4].wait()
 
-    wait_bytes(sum_c.at[pl.ds(0, n_cand // 2 - 1)], recv_c.at[0])
-    cand_moment[r, core] = jnp.sum(sum_c[...], axis=0)
     wait_bytes(sum_r.at[pl.ds(0, n_ref - 1)], recv_r.at[0])
     my_slice = ref_moment.at[pl.ds(pl.multiple_of(first_r, width_r), width_r)]
     my_slice[...] = jnp.sum(sum_r[...], axis=0)
-
     for_all(
         lambda device: remote(
             my_slice, my_slice, send_c.at[1], recv_c.at[1], device
         ).start(),
+        None,
+        (0,),
+    )
+    wait_bytes(sum_c.at[pl.ds(0, n_cand // 2 - 1)], recv_c.at[0])
+    cand_moment[r, core] = jnp.sum(sum_c[...], axis=0)
+    for_all(
+        None,
         lambda device: remote(
             cand_moment.at[r, core],
             cand_moment.at[r, core],
@@ -258,10 +277,8 @@
     wait_bytes(ref_moment.at[pl.ds(0, half - width_r)], recv_c.at[1])
     hand_r = remote(my_half, my_half, pair_send.at[1], pair_recv.at[1], to_c(0, 0, 1))
     hand_r.start()
-    wait_bytes(cand_moment.at[pl.ds(0, n_ref - 1), core], recv_r.at[1])
     mine = cand_moment.at[:, pl.ds(core, 1)]
     hand_c = remote(mine, mine, pair_send.at[2], pair_recv.at[2], to_c(0, 0, 1))
-    hand_c.start()
 
     weights_row = weights[...]
     weights_inverse = 1.0 / weights_row
@@ -289,6 +306,8 @@
         kc[here, :] = product(cf_high, cf_low, core, here, right)
     tops = jnp.zeros((8, LANES), F32)
     hand_r.wait_recv()
+    wait_bytes(cand_moment.at[pl.ds(0, n_ref - 1), core], recv_r.at[1])
+    hand_c.start()
     other = ref_moment[pl.ds(pl.multiple_of(sibling * half, half), half), :]
     right = right_side(other)
     for here in tiles(rows_c, step_c):
@@ -307,6 +326,21 @@
         kr[here, :] = grad
         tops = peak(tops, grad)
     local = jnp.max(tops, axis=0, keepdims=True)
+
+    def sent(slot):
+        if slot == 0:
+            pair.wait_send()
+            wait_bytes(sum_c.at[pl.ds(0, n_cand // 2 - 1)], send_c.at[0])
+            wait_bytes(sum_r.at[pl.ds(0, n_ref - 1)], send_r.at[0])
+        elif slot == 1:
+            hand_r.wait_send()
+            hand_c.wait_send()
+            wait_bytes(ref_moment.at[pl.ds(0, half - width_r)], send_c.at[1])
+            wait_bytes(cand_moment.at[pl.ds(0, n_ref - 1), core], send_r.at[1])
+
+    def rows_sent(slot):
+        wait_bytes(in_c.at[slot, pl.ds(0, n_cand - 1)], send_c.at[2 + slot])
+        wait_bytes(in_r.at[slot, pl.ds(0, n_ref - 1)], send_r.at[2 + slot])
 
     def exchange(slot, row_c, row_r):
         out_row[slot, 0] = row_c
@@ -330,6 +364,9 @@
         )
         in_c[slot, c] = row_c
         in_r[slot, r] = row_r
+        sent(slot)
+        if slot > 0:
+            rows_sent(slot - 1)
         wait_bytes(in_c.at[slot, pl.ds(0, n_cand - 1)], recv_c.at[2 + slot])
         wait_bytes(in_r.at[slot, pl.ds(0, n_ref - 1)], recv_r.at[2 + slot])
         return in_c[slot], in_r[slot]
@@ -369,8 +406,8 @@
         part_mass_c = row_pass(kc, cp, scale_c, first, scaled_cand if last else None)
         part_mass_r = row_pass(kr, rp, scale_r, first, scaled_ref if last else None)
         masses_c, masses_r = exchange(1 + i, part_mass_c, part_mass_r)
-        mass_c = jnp.sum(masses_c, axis=0) * (1.0 / (rows_c * n_cand))
-        mass_r = jnp.sum(masses_r, axis=0) * (1.0 / (rows_r * n_ref))
+        mass_c = add_up(masses_c) * (1.0 / (rows_c * n_cand))
+        mass_r = add_up(masses_r) * (1.0 / (rows_r * n_ref))
         new_weights = cube_root(kernel_weights * scale_c * mass_c * scale_r * mass_r)
         scale_c = new_weights / mass_c
         scale_r = new_weights / mass_r
@@ -379,16 +416,7 @@
     rows_out[1:2] = scale_c
     rows_out[2:3] = scale_r
 
-    pair.wait_send()
-    hand_r.wait_send()
-    hand_c.wait_send()
-    wait_bytes(sum_c.at[pl.ds(0, n_cand // 2 - 1)], send_c.at[0])
-    wait_bytes(sum_r.at[pl.ds(0, n_ref - 1)], send_r.at[0])
-    wait_bytes(ref_moment.at[pl.ds(0, half - width_r)], send_c.at[1])
-    wait_bytes(cand_moment.at[pl.ds(0, n_ref - 1), core], send_r.at[1])
-    for slot in range(1 + ITERS):
-        wait_bytes(in_c.at[slot, pl.ds(0, n_cand - 1)], send_c.at[2 + slot])
-        wait_bytes(in_r.at[slot, pl.ds(0, n_ref - 1)], send_r.at[2 + slot])
+    rows_sent(ITERS)
 
 
 def finish(
@@ -396,9 +424,12 @@
 ):
     rows_c, rows_r = c.shape[0], r.shape[0]
     pieces = [
-        (scaled_cand, c, new_cand_plan, 1, pl.ds(i * rows_c // 2, rows_c // 2))
+        (scaled_cand, c, new_cand_plan, 1, pl.ds(i * rows_c // 4, rows_c // 4))
+        for i in range(4)
+    ] + [
+        (scaled_ref, r, new_ref_plan, 2, pl.ds(i * rows_r // 2, rows_r // 2))
         for i in range(2)
-    ] + [(scaled_ref, r, new_ref_plan, 2, pl.ds(0, rows_r))]
+    ]
     stores = [
         pltpu.make_async_copy(rows.at[pl.ds(0, 1)], new_weights, sems.at[len(pieces)])
     ]
@@ -482,7 +513,7 @@
         scratch_shapes=[
             pltpu.VMEM((rows_c, rank), F32),
             pltpu.VMEM((rows_r, rank), F32),
-            pltpu.SemaphoreType.DMA((4,)),
+            pltpu.SemaphoreType.DMA((7,)),
         ],
         compiler_params=pltpu.CompilerParams(vmem_limit_bytes=16 * 2**20),
     )(

time: 55.1 us -> 53.9 us (0.978)
  Pallas kernels: 54.3 us -> 53.1 us
    pallas_call x1, Pallas kernels: 53.4 us -> 52.1 us  [on_device(): pl.pallas_call(functools.partial(kernel, n_cand, n_ref), out_shape=(pltpu...]
where the time goes in v4:
time: 53.9 us; the launch traced here: 53.7 us
  Pallas kernels  53.1 us (99%)
  between operations  0.64 us (1%)
    pallas_call x1, Pallas kernels, on_device(): pl.pallas_call(functools.partial(kernel, n_cand, n_ref), out_shape=(pltpu...  52.1 us

profile of v4, /device:TPU:1, one launch (start us, length us, event | category | flops | bytes accessed | tf_op | source)
XLA Modules:
  0.0 53.7 jit_solution(7589374576630435742)
XLA Ops:
  0.6 52.1 %shard_map.76 = (f32[1024,128]{1,0:T(8,128)S(1)}, f32[512,128]{1,0:T(8,128)S(1)}, f32[8,128]{1,0:T(8,128)S(1)}) custom-call(f32[1024,512]{1,0:T(8,128)} %cand_factor.1, f32[512,512]{1,0:T(8,128)} %ref_factor.1, f32[1024,128]{1,0:T(8,128)} %cand_plan.1, f32[512,128]{1,0:T(8,128)} %ref_plan.1, f32[1,128]{1,0:T(1,128)} %bitcast.2), custom_call_target="tpu_custom_call" | custom-call | tf_op jit(solution)/shard_map/pallas_call | solution.py:459
  52.8 0.9 %shard_map.77 = (f32[1024,128]{1,0:T(8,128)}, f32[512,128]{1,0:T(8,128)}, f32[1,128]{1,0:T(1,128)}) custom-call(f32[1024,128]{1,0:T(8,128)S(1)} %get-tuple-element.9.scaled_cand, f32[512,128]{1,0:T(8,128)S(1)} %get-tuple-element.10.scaled_ref, f32[8,128]{1,0:T(8,128)S(1)} %get-tuple-element.11.rows), custom_call_target="tpu_custom_call" | custom-call | tf_op jit(solution)/shard_map/pallas_call | solution.py:504

commit v5 on v4

--- a/solution.py
+++ b/solution.py
@@ -113,10 +113,6 @@
     part = width_c // 2
     sibling = 1 - core
 
-    def away(step, size):
-        turn = lax.rem(step, 2) * 2 - 1
-        return lax.rem(size // 2 + turn * ((step + 1) // 2) + size, size)
-
     def to_c(flip, offset_y, flip_core):
         new_x = lax.rem(x_lo + flip, 2)
         new_core = lax.rem(core + flip_core, 2)
@@ -127,25 +123,19 @@
         return (new_c, lax.rem(z + offset_z, n_z) * 2 + lax.rem(x_hi + flip, 2))
 
     def for_all(visit_c, visit_r, cores):
-        def body(step, _):
-            offset_y = away(step, n_y)
-            for flip in (1, 0):
-                if visit_c:
-                    for flip_core in cores:
-                        visit_c(to_c(flip, offset_y, flip_core))
-                if visit_r and n_z == n_y:
-                    visit_r(to_r(flip, offset_y))
-            return 0
-
-        lax.fori_loop(0, n_y - 1, body, 0)
+        def ring(size):
+            order = sorted(range(1, size), key=lambda d: -min(d, size - d))
+            return [(d, flip) for d in order for flip in (1, 0)]
+
+        for offset, flip in ring(n_y):
+            if visit_c:
+                for flip_core in cores:
+                    visit_c(to_c(flip, offset, flip_core))
+            if visit_r and n_z == n_y:
+                visit_r(to_r(flip, offset))
         if visit_r and n_z != n_y:
-
-            def body_r(step, _):
-                for flip in (1, 0):
-                    visit_r(to_r(flip, away(step, n_z)))
-                return 0
-
-            lax.fori_loop(0, n_z - 1, body_r, 0)
+            for offset, flip in ring(n_z):
+                visit_r(to_r(flip, offset))
         if visit_c:
             for flip_core in cores:
                 visit_c(to_c(1, 0, flip_core))

time: 53.9 us -> 53.8 us (level)
  no operation moved by 1% of the time
where the time goes in v5:
time: 53.8 us; the launch traced here: 53.6 us
  Pallas kernels  53 us (99%)
  between operations  0.64 us (1%)
    pallas_call x1, Pallas kernels, on_device(): pl.pallas_call(functools.partial(kernel, n_cand, n_ref), out_shape=(pltpu...  52 us

profile of v5, /device:TPU:1, one launch (start us, length us, event | category | flops | bytes accessed | tf_op | source)
XLA Modules:
  0.0 53.6 jit_solution(5133781245514209261)
XLA Ops:
  0.6 52.0 %shard_map.76 = (f32[1024,128]{1,0:T(8,128)S(1)}, f32[512,128]{1,0:T(8,128)S(1)}, f32[8,128]{1,0:T(8,128)S(1)}) custom-call(f32[1024,512]{1,0:T(8,128)} %cand_factor.1, f32[512,512]{1,0:T(8,128)} %ref_factor.1, f32[1024,128]{1,0:T(8,128)} %cand_plan.1, f32[512,128]{1,0:T(8,128)} %ref_plan.1, f32[1,128]{1,0:T(1,128)} %bitcast.2), custom_call_target="tpu_custom_call" | custom-call | tf_op jit(solution)/shard_map/pallas_call | solution.py:449
  52.7 0.9 %shard_map.77 = (f32[1024,128]{1,0:T(8,128)}, f32[512,128]{1,0:T(8,128)}, f32[1,128]{1,0:T(1,128)}) custom-call(f32[1024,128]{1,0:T(8,128)S(1)} %get-tuple-element.9.scaled_cand, f32[512,128]{1,0:T(8,128)S(1)} %get-tuple-element.10.scaled_ref, f32[8,128]{1,0:T(8,128)S(1)} %get-tuple-element.11.rows), custom_call_target="tpu_custom_call" | custom-call | tf_op jit(solution)/shard_map/pallas_call | solution.py:494

commit v6 on v5

--- a/solution.py
+++ b/solution.py
@@ -374,17 +374,26 @@
     scale_c = jnp.ones((1, LANES), F32)
     scale_r = jnp.ones((1, LANES), F32)
 
-    def row_pass(k, plan, scale, first, to):
+    def row_sums(block, by_matmul):
+        if not by_matmul:
+            return jnp.sum(block, axis=1, keepdims=True)
+        high, low = split(block)
+        ones = jnp.ones((LANES, LANES), BF16)
+        return jnp.dot(high, ones, preferred_element_type=F32) + jnp.dot(
+            low, ones, preferred_element_type=F32
+        )
+
+    def row_pass(k, plan, scale, first, to, by_matmul):
         rows = k.shape[0]
         mass = jnp.zeros((8, LANES), F32)
         for here in tiles(rows, min(rows, 128)):
             if first:
                 block = plan[here, :] * jnp.exp(k[here, :] * factor)
                 k[here, :] = block
-                total = jnp.sum(block, axis=1, keepdims=True)
+                total = row_sums(block, by_matmul)
             else:
                 block = k[here, :]
-                total = jnp.sum(block * scale, axis=1, keepdims=True)
+                total = row_sums(block * scale, by_matmul)
             scaled = block * (LANES / total)
             if to is not None:
                 to[here, :] = scaled
@@ -393,8 +402,12 @@
 
     for i in range(ITERS):
         first, last = i == 0, i == ITERS - 1
-        part_mass_c = row_pass(kc, cp, scale_c, first, scaled_cand if last else None)
-        part_mass_r = row_pass(kr, rp, scale_r, first, scaled_ref if last else None)
+        part_mass_c = row_pass(
+            kc, cp, scale_c, first, scaled_cand if last else None, False
+        )
+        part_mass_r = row_pass(
+            kr, rp, scale_r, first, scaled_ref if last else None, True
+        )
         masses_c, masses_r = exchange(1 + i, part_mass_c, part_mass_r)
         mass_c = add_up(masses_c) * (1.0 / (rows_c * n_cand))
         mass_r = add_up(masses_r) * (1.0 / (rows_r * n_ref))

time: 53.8 us -> 53.7 us (level)
  no operation moved by 1% of the time
where the time goes in v6:
time: 53.7 us; the launch traced here: 53.5 us
  Pallas kernels  52.9 us (99%)
  between operations  0.64 us (1%)
    pallas_call x1, Pallas kernels, on_device(): pl.pallas_call(functools.partial(kernel, n_cand, n_ref), out_shape=(pltpu...  52 us

profile of v6, /device:TPU:1, one launch (start us, length us, event | category | flops | bytes accessed | tf_op | source)
XLA Modules:
  0.0 53.5 jit_solution(12148200488760807887)
XLA Ops:
  0.6 52.0 %shard_map.76 = (f32[1024,128]{1,0:T(8,128)S(1)}, f32[512,128]{1,0:T(8,128)S(1)}, f32[8,128]{1,0:T(8,128)S(1)}) custom-call(f32[1024,512]{1,0:T(8,128)} %cand_factor.1, f32[512,512]{1,0:T(8,128)} %ref_factor.1, f32[1024,128]{1,0:T(8,128)} %cand_plan.1, f32[512,128]{1,0:T(8,128)} %ref_plan.1, f32[1,128]{1,0:T(1,128)} %bitcast.2), custom_call_target="tpu_custom_call" | custom-call | tf_op jit(solution)/shard_map/pallas_call | solution.py:462
  52.6 0.9 %shard_map.77 = (f32[1024,128]{1,0:T(8,128)}, f32[512,128]{1,0:T(8,128)}, f32[1,128]{1,0:T(1,128)}) custom-call(f32[1024,128]{1,0:T(8,128)S(1)} %get-tuple-element.9.scaled_cand, f32[512,128]{1,0:T(8,128)S(1)} %get-tuple-element.10.scaled_ref, f32[8,128]{1,0:T(8,128)S(1)} %get-tuple-element.11.rows), custom_call_target="tpu_custom_call" | custom-call | tf_op jit(solution)/shard_map/pallas_call | solution.py:507
